TPU v7x, 32 devices: a whole 2x2x4 slice. The times are simulated.
32 devices in a mesh: dp: 8 (over z, core), tensor: 4 (over y, x).
Axes of the slice: x: 2, y: 2, z: 4, core: 2. Of those that a mesh axis runs over, the one named last changes fastest.
Arguments:
- acts: bfloat16 [1024, 8192], P('dp', 'tensor'), may hold values from -6 to 6
- grad_out: bfloat16 [1024, 14336], P('dp', 'tensor'), may hold values from -6 to 6
- proj_t: bfloat16 [512, 8192], P(None, 'tensor'), may hold values from -6 to 6
- first_moment: float32 [512, 14336], P('dp', 'tensor'), may hold values from -0.15625 to 0.15625
- second_moment: float32 [512, 14336], P('dp', 'tensor'), may hold values from 1e-05 to 0.001
Outputs:
- adam_step: float32 [512, 14336], P('dp', 'tensor')
- new_proj_t: float32 [512, 8192], P('dp', 'tensor')
All inputs are finite; a program needn't handle non-finite values.
Results may differ from a plain program's by a relative error of at most 0.023.
Values may be sent and summed in bfloat16 or wider, within the bound.
A program may use at most 64 MiB of HBM per device.

v0:
```python
import jax
import jax.numpy as jnp
from jax import lax
from jax.sharding import PartitionSpec as P

D = 8192


def contract_rows(left, right):
    return lax.dot_general(
        left, right, (((0,), (0,)), ((), ())), preferred_element_type=jnp.float32
    )


def contract_cols(left, right):
    return lax.dot_general(
        left, right, (((1,), (1,)), ((), ())), preferred_element_type=jnp.float32
    )


def local(acts, grad_out, proj_t, first_moment, second_moment):
    tok_rows = acts.shape[0]
    total_tokens = tok_rows * lax.axis_size("dp")
    rank_rows = first_moment.shape[0]
    inv_root = 1.0 / jnp.sqrt(jnp.float32(D))
    row_start = lax.axis_index("dp") * rank_rows
    local_coords = contract_cols(acts, proj_t) * inv_root
    coords = lax.psum(local_coords.astype(jnp.bfloat16), "tensor")
    picked = coords
    grad_part = lax.psum_scatter(
        contract_rows(picked, grad_out) / total_tokens, "dp", scatter_dimension=0, tiled=True
    )
    low_part = grad_part.astype(jnp.bfloat16)
    piece = lax.all_gather(low_part, "dp", axis=0, tiled=True)
    joined = jnp.concatenate(
        [contract_cols(grad_out, piece), contract_cols(low_part, piece)], axis=0
    )
    back_part = joined[:tok_rows]
    cross_part = joined[tok_rows:]
    moment_one = 0.9 * first_moment + 0.1 * grad_part
    moment_two = 0.999 * second_moment + 0.001 * grad_part * grad_part
    adam_step = moment_one / (1.0 - 0.9**10) / (jnp.sqrt(moment_two / (1.0 - 0.999**10)) + 1e-08)
    back, cross = (
        lax.psum(back_part.astype(jnp.bfloat16), "tensor").astype(jnp.float32),
        lax.psum(cross_part.astype(jnp.bfloat16), "tensor").astype(jnp.float32),
    )
    back_low = back.astype(jnp.bfloat16)
    picked = back_low
    pull = lax.psum_scatter(
        contract_rows(picked, acts) / total_tokens, "dp", scatter_dimension=0, tiled=True
    )
    proj_wide = proj_t.astype(jnp.float32)
    own_rows = lax.dynamic_slice_in_dim(proj_wide, row_start, rank_rows, 0)
    correction = jnp.dot(cross, proj_wide, precision=lax.Precision.HIGHEST)
    new_proj_t = own_rows + jnp.sqrt(jnp.float32(D)) * pull - correction
    return (adam_step, new_proj_t)


def solution(mesh):
    placed = (
        P("dp", "tensor"),
        P("dp", "tensor"),
        P(None, "tensor"),
        P("dp", "tensor"),
        P("dp", "tensor"),
    )
    return jax.shard_map(
        local,
        mesh=mesh,
        in_specs=placed,
        out_specs=(P("dp", "tensor"), P("dp", "tensor")),
        check_vma=False,
    )
```

profile of v0, /device:TPU:1, one launch (start us, length us, event | category | flops | bytes accessed | tf_op | source)
XLA Modules:
  0.0 292.8 jit_solution(29727122650589353)
XLA Ops:
  7.2 0.0 copy-start
  7.2 0.0 all-reduce.4.cloned.1.call-start
  7.2 3.3 %fusion = bf16[128,512]{1,0:T(8,128)(2,1)} fusion(bf16[128,2048]{1,0:T(8,128)(2,1)} %param.5, bf16[512,2048]{1,0:T(8,128)(2,1)} %param.7), kind=kOutput, calls=%fused_computation.5 | convolution fusion | flops 268566528 | bytes 2752512 | tf_op jit(solution)/shard_map/dot_general | solution.py:16
  10.5 0.0 all-reduce.4.cloned.1.call-update
  10.6 0.0 reduce-scatter.3.cloned.1.call-start
  10.6 44.6 %all-reduce.4.cloned.1.call-done = bf16[128,512]{1,0:T(8,128)(2,1)} async-done(((bf16[128,512]{1,0:T(8,128)(2,1)}), bf16[128,512]{1,0:T(8,128)(2,1)}) %all-reduce.4.cloned.1.call-update) | async-done | bytes 131088 | tf_op jit(solution)/shard_map/psum | solution.py:28
  55.2 0.0 copy-done
  55.2 5.0 %convolution_multiply_fusion = f32[512,3584]{1,0:T(8,128)} fusion(bf16[128,512]{1,0:T(8,128)(2,1)} %all-reduce.4.cloned.1.call-done, bf16[128,3584]{1,0:T(8,128)(2,1)S(1)} %copy-done), kind=kOutput, calls=%fused_computation | convolution fusion | flops 471597056 | bytes 8388608 | tf_op jit(solution)/shard_map/dot_general | solution.py:10
  60.2 0.0 copy-start.4
  60.2 0.0 reduce-scatter.3.cloned.1.call-update
  60.2 0.0 all-gather.2.cloned.1.call-start
  60.3 78.1 %reduce-scatter.3.cloned.1.call-done = f32[64,3584]{1,0:T(8,128)} async-done(((f32[512,3584]{1,0:T(8,128)}), f32[64,3584]{1,0:T(8,128)}) %reduce-scatter.3.cloned.1.call-update) | async-done | bytes 917520 | tf_op jit(solution)/shard_map/reduce_scatter | solution.py:30
  138.3 0.0 copy-done.4
  138.3 0.0 copy-done.5
  138.3 3.1 %fusion.7 = (bf16[64,3584]{1,0:T(8,128)(2,1)}, f32[64,3584]{1,0:T(8,128)}) fusion(f32[64,3584]{1,0:T(8,128)} %reduce-scatter.3.cloned.1.call-done, f32[64,3584]{1,0:T(8,128)S(1)} %copy-done.4, f32[64,3584]{1,0:T(8,128)S(1)} %copy-done.5), kind=kLoop, calls=%fused_computation.14 | loop fusion | flops 2752512 | bytes 4128768 | tf_op jit(solution)/shard_map/convert_element_type | solution.py:33
  141.4 0.0 all-gather.2.cloned.1.call-update
  141.5 0.0 copy-start.3
  141.5 0.0 all-reduce.6.cloned.1.call-start
  141.5 43.6 %all-gather.2.cloned.1.call-done = bf16[512,3584]{1,0:T(8,128)(2,1)} async-done(((bf16[64,3584]{1,0:T(8,128)(2,1)}), bf16[512,3584]{1,0:T(8,128)(2,1)}) %all-gather.2.cloned.1.call-update) | async-done | bytes 3670032 | tf_op jit(solution)/shard_map/all_gather | solution.py:34
  185.1 4.2 %convolution_convert_fusion.1 = bf16[64,512]{1,0:T(8,128)(2,1)} fusion(bf16[64,3584]{1,0:T(8,128)(2,1)} %get-tuple-element.4, bf16[512,3584]{1,0:T(8,128)(2,1)} %all-gather.2.cloned.1.call-done), kind=kOutput, calls=%fused_computation.8 | convolution fusion | flops 234913792 | bytes 4194304 | tf_op jit(solution)/shard_map/dot_general | solution.py:16
  189.3 0.0 copy-done.2
  189.3 1.8 fusion.1
  191.0 0.0 all-reduce.6.cloned.1.call-update
  191.0 0.0 reduce-scatter.5.cloned.1.call-start
  191.1 40.7 %all-reduce.6.cloned.1.call-done = (bf16[64,512]{1,0:T(8,128)(2,1)}, bf16[128,512]{0,1:T(8,128)(2,1)}) async-done(((bf16[64,512]{1,0:T(8,128)(2,1)}, bf16[128,512]{0,1:T(8,128)(2,1)}), (bf16[64,512]{1,0:T(8,128)(2,1)}, bf16[128,512]{0,1:T(8,128)(2,1)})) %all-reduce.6.cloned.1.call-update) | async-done | bytes 196624 | tf_op jit(solution)/shard_map/psum | solution.py:45
  231.8 0.0 copy-done.3
  231.8 3.7 %convolution_multiply_fusion.1 = f32[512,2048]{1,0:T(8,128)} fusion(bf16[128,512]{0,1:T(8,128)(2,1)} %get-tuple-element.3, bf16[128,2048]{1,0:T(8,128)(2,1)S(1)} %copy-done.3), kind=kOutput, calls=%fused_computation.1 | convolution fusion | flops 269484032 | bytes 4849664 | tf_op jit(solution)/shard_map/dot_general | solution.py:10
  235.5 0.0 reduce-scatter.5.cloned.1.call-update
  235.5 48.4 %reduce-scatter.5.cloned.1.call-done = f32[64,2048]{1,0:T(8,128)} async-done(((f32[512,2048]{1,0:T(8,128)}), f32[64,2048]{1,0:T(8,128)}) %reduce-scatter.5.cloned.1.call-update) | async-done | bytes 524304 | tf_op jit(solution)/shard_map/reduce_scatter | solution.py:49
  283.9 0.0 copy-done.1
  284.0 0.0 copy-done.6
  284.0 2.3 convolution_subtract_fusion
  (4 shorter events, 0.0 us)
Async XLA Ops:
  7.2 48.0 %copy-start = (bf16[128,3584]{1,0:T(8,128)(2,1)S(1)}, bf16[128,3584]{1,0:T(8,128)(2,1)}, u32[]{:S(2)}) copy-start(bf16[128,3584]{1,0:T(8,128)(2,1)} %param.6) | copy-start | bytes 2752516
  7.2 48.0 %all-reduce.4.cloned.1.call-start = ((), (), s32[]{:S(2)}) async-start(), calls=%async_computation.2 | async-start | bytes 262144 | tf_op jit(solution)/shard_map/psum | solution.py:28
  10.6 127.8 %reduce-scatter.3.cloned.1.call-start = ((), (), s32[]{:S(2)}) async-start(), calls=%async_computation.3 | async-start | bytes 8257536 | tf_op jit(solution)/shard_map/reduce_scatter | solution.py:30
  60.2 78.2 %copy-start.4 = (f32[64,3584]{1,0:T(8,128)S(1)}, f32[64,3584]{1,0:T(8,128)}, u32[]{:S(2)}) copy-start(f32[64,3584]{1,0:T(8,128)} %param.9) | copy-start | bytes 2752516
  60.2 78.2 %copy-start.5 = (f32[64,3584]{1,0:T(8,128)S(1)}, f32[64,3584]{1,0:T(8,128)}, u32[]{:S(2)}) copy-start(f32[64,3584]{1,0:T(8,128)} %param.8) | copy-start | bytes 2752516
  60.2 124.9 %all-gather.2.cloned.1.call-start = ((), (), s32[]{:S(2)}) async-start(), calls=%async_computation.4 | async-start | bytes 4128768 | tf_op jit(solution)/shard_map/all_gather | solution.py:34
  141.5 90.4 %copy-start.3 = (bf16[128,2048]{1,0:T(8,128)(2,1)S(1)}, bf16[128,2048]{1,0:T(8,128)(2,1)}, u32[]{:S(2)}) copy-start(bf16[128,2048]{1,0:T(8,128)(2,1)} %param.5) | copy-start | bytes 1572868
  141.5 90.3 %all-reduce.6.cloned.1.call-start = ((), (), s32[]{:S(2)}) async-start(), calls=%async_computation.6 | async-start | bytes 393216 | tf_op jit(solution)/shard_map/psum | solution.py:45
  185.1 4.2 %copy-start.2 = (bf16[512,3584]{1,0:T(8,128)(2,1)S(1)}, bf16[512,3584]{1,0:T(8,128)(2,1)}, u32[]{:S(2)}) copy-start(bf16[512,3584]{1,0:T(8,128)(2,1)} %all-gather.2.cloned.1.call-done) | copy-start | bytes 11010052
  191.0 92.9 %reduce-scatter.5.cloned.1.call-start = ((), (), s32[]{:S(2)}) async-start(), calls=%async_computation.5 | async-start | bytes 4718592 | tf_op jit(solution)/shard_map/reduce_scatter | solution.py:49
  231.8 52.1 %copy-start.1 = (bf16[512,2048]{1,0:T(8,128)(2,1)S(1)}, bf16[512,2048]{1,0:T(8,128)(2,1)}, u32[]{:S(2)}) copy-start(bf16[512,2048]{1,0:T(8,128)(2,1)} %param.7) | copy-start | bytes 6291460
  235.5 48.4 %copy-start.6 = (bf16[64,512]{1,0:T(8,128)(2,1)S(1)}, bf16[64,512]{1,0:T(8,128)(2,1)}, u32[]{:S(2)}) copy-start(bf16[64,512]{1,0:T(8,128)(2,1)} %get-tuple-element.2) | copy-start | bytes 196612
Sparse Core Ops, SparseCore 0:
  11.5 43.6 all-reduce.3
  60.3 77.9 reduce-scatter.2
  141.6 43.4 all-gather.1
  191.2 40.6 all-reduce.5
  235.7 48.2 reduce-scatter.4
where the time goes:
time: 296 us; the launch traced here: 293 us
  waiting for transfers between devices  255 us (86%)
  matrix products  20.2 us (7%)
  between operations  13.8 us (5%)
  other arithmetic  3.1 us (1%)
    reduce_scatter x1, waiting for transfers between devices, local(): lax.psum_scatter(contract_rows(picked, grad_out) / total_tokens, 'dp', sc...  78.1 us
    reduce_scatter x1, waiting for transfers between devices, local(): lax.psum_scatter(contract_rows(picked, acts) / total_tokens, 'dp', scatte...  48.4 us
    psum x1, waiting for transfers between devices, local(): coords = lax.psum(local_coords.astype(jnp.bfloat16), 'tensor')  44.6 us
    all_gather x1, waiting for transfers between devices, local(): piece = lax.all_gather(low_part, 'dp', axis=0, tiled=True)  43.6 us
    psum x1, waiting for transfers between devices, local(): lax.psum(cross_part.astype(jnp.bfloat16), 'tensor').astype(jnp.float32)  40.7 us
    dot_general x3, matrix products, contract_cols(): lax.dot_general(left, right, (((1,), (1,)), ((), ())), preferred_element_...  9.25 us
    dot_general x2, matrix products, contract_rows(): lax.dot_general(left, right, (((0,), (0,)), ((), ())), preferred_element_...  8.68 us
  transfers between devices with their start and end apart: 5, of which 5 were waited for; matrix products, arithmetic and copies ran while one was open for 0% of the time, Pallas kernels for 0%

commit v1 on v0

v1 whole, which is shorter than its diff:
```python
import functools

import jax
import jax.numpy as jnp
from jax import lax
from jax.experimental import pallas as pl
from jax.experimental.pallas import tpu as pltpu
from jax.sharding import PartitionSpec as P

MESH = pl.DeviceIdType.MESH
ANY = pl.BlockSpec(memory_space=pl.ANY)
VMEM = pl.BlockSpec(memory_space=pltpu.VMEM)


def contract_rows(left, right):
    return lax.dot_general(
        left, right, (((0,), (0,)), ((), ())), preferred_element_type=jnp.float32
    )


def contract_cols(left, right):
    return lax.dot_general(
        left, right, (((1,), (1,)), ((), ())), preferred_element_type=jnp.float32
    )


def place():
    dp = lax.axis_index("dp")
    return dp, lax.div(dp, 2), lax.rem(dp, 2), lax.axis_index("tensor")


def greet(n_dp, n_ten):
    dp, _, _, ten = place()
    barrier = pltpu.get_barrier_semaphore()
    for k in range(1, n_dp):
        pl.semaphore_signal(
            barrier, inc=1, device_id=(lax.rem(dp + k, n_dp), ten), device_id_type=MESH
        )
    for k in range(1, n_ten):
        pl.semaphore_signal(
            barrier, inc=1, device_id=(dp, lax.rem(ten + k, n_ten)), device_id_type=MESH
        )
    pl.semaphore_wait(barrier, n_dp + n_ten - 2)


def send(src, dst, sems, k, device):
    copy = pltpu.make_async_remote_copy(
        src_ref=src,
        dst_ref=dst,
        send_sem=sems.at[0, k],
        recv_sem=sems.at[1, k],
        device_id=device,
        device_id_type=MESH,
    )
    copy.start()
    return copy


def start_swap(src, dst, sems, n_dp):
    dp, _, _, ten = place()
    copies = []
    for k in range(1, n_dp):
        peer = lax.rem(dp + k, n_dp)
        copies.append(send(src.at[peer], dst.at[dp], sems, k, (peer, ten)))
    own = pltpu.make_async_copy(src.at[dp], dst.at[dp], sems.at[0, 0])
    own.start()
    return copies + [own]


def wait_all(copies):
    for copy in copies:
        copy.wait()


def reduce_stage(src, got, sems, me, n, device):
    copies = []
    for k in range(1, n):
        peer = lax.rem(me + k, n)
        copies.append(send(src.at[peer], got.at[k], sems, k, device(peer)))
    total = src[me].astype(jnp.float32)
    for k in range(1, n):
        copies[k - 1].wait()
        total = total + got[k].astype(jnp.float32)
    return total


def gather_stages(full, sems_z, sems_t, sems_c, n_z, n_ten):
    _, z, c, ten = place()
    copies = []
    mine = full.at[c, ten, z]
    for k in range(1, n_z):
        peer = lax.rem(z + k, n_z)
        copies.append(send(mine, mine, sems_z, k, (peer * 2 + c, ten)))
    wait_all(copies)
    copies = []
    mine = full.at[c, ten]
    for k in range(1, n_ten):
        peer = lax.rem(ten + k, n_ten)
        copies.append(send(mine, mine, sems_t, k, (z * 2 + c, peer)))
    wait_all(copies)
    mine = full.at[c]
    send(mine, mine, sems_c, 1, (z * 2 + 1 - c, ten)).wait()


def coords_kernel(n_dp, n_ten, g8, part, g_all, full_out, full, got, s_g, s_r, s_z, s_t, s_c):
    n_z = n_dp // 2
    dp, z, c, ten = place()
    greet(n_dp, n_ten)
    total = reduce_stage(part, got, s_r, ten, n_ten, lambda p: (dp, p))
    swaps = start_swap(g8, g_all, s_g, n_dp)
    full[c, ten, z] = total.astype(full.dtype)
    gather_stages(full, s_z, s_t, s_c, n_z, n_ten)
    out = pltpu.make_async_copy(full, full_out, s_c.at[0, 0])
    out.start()
    wait_all(swaps + [out])


def back_kernel(
    n_dp, n_ten, low8, a8, part, low_all, a_all, full_out,
    full, got_c, mid_c, got_t, mid_t, got_z, s_l, s_a, s_rc, s_rt, s_rz, s_z, s_t, s_c,
):
    n_z = n_dp // 2
    dp, z, c, ten = place()
    greet(n_dp, n_ten)
    mid_c[...] = reduce_stage(
        part, got_c, s_rc, c, 2, lambda p: (z * 2 + p, ten)
    ).astype(mid_c.dtype)
    swaps = start_swap(low8, low_all, s_l, n_dp) + start_swap(a8, a_all, s_a, n_dp)
    mid_t[...] = reduce_stage(
        mid_c, got_t, s_rt, ten, n_ten, lambda p: (dp, p)
    ).astype(mid_t.dtype)
    total = reduce_stage(mid_t, got_z, s_rz, z, n_z, lambda p: (p * 2 + c, ten))
    full[c, ten, z] = total.astype(full.dtype)
    gather_stages(full, s_z, s_t, s_c, n_z, n_ten)
    out = pltpu.make_async_copy(full, full_out, s_c.at[0, 0])
    out.start()
    wait_all(swaps + [out])


def swap_kernel(n_dp, src, dst, sems):
    greet(n_dp, 1)
    wait_all(start_swap(src, dst, sems, n_dp))


def pairs(n):
    return pltpu.SemaphoreType.DMA((2, n))


def params(which):
    return pltpu.CompilerParams(
        collective_id=which, has_side_effects=True, vmem_limit_bytes=32 * 2**20
    )


def like(shape, dtype=jnp.bfloat16):
    return jax.ShapeDtypeStruct(shape, dtype)


def to_blocks(x, n, width):
    rows, cols = x.shape
    x = x.reshape(rows, n, cols // n).transpose(1, 0, 2)
    return jnp.pad(x, ((0, 0), (0, 0), (0, width - cols // n)))


def direct(n_dp, n_ten, acts, grad_out, proj_t, first_moment, second_moment):
    n_z = n_dp // 2
    tok_rows, width = acts.shape
    hidden = grad_out.shape[1]
    rank = proj_t.shape[0]
    rank_rows = first_moment.shape[0]
    tokens = tok_rows * n_dp
    dim = jnp.float32(width * n_ten)
    bf16 = jnp.bfloat16
    h_blk = hidden // n_dp
    h_pad = -(-h_blk // 128) * 128
    w_blk = width // n_dp
    sub = tok_rows // n_ten

    part = (contract_cols(acts, proj_t) * (1.0 / jnp.sqrt(dim))).astype(bf16)
    g8 = to_blocks(grad_out, n_dp, h_pad)
    g_all, coords = pl.pallas_call(
        functools.partial(coords_kernel, n_dp, n_ten),
        out_shape=(like(g8.shape), like((2, n_ten, n_z, sub, rank))),
        in_specs=[ANY, VMEM],
        out_specs=(ANY, ANY),
        scratch_shapes=[
            pltpu.VMEM((2, n_ten, n_z, sub, rank), bf16),
            pltpu.VMEM((n_ten, sub, rank), bf16),
            pairs(n_dp), pairs(n_ten), pairs(n_z), pairs(n_ten), pairs(2),
        ],
        compiler_params=params(0),
    )(g8, part.reshape(n_ten, sub, rank))
    coords = coords.transpose(2, 0, 1, 3, 4).reshape(tokens, rank)
    g_all = g_all.reshape(tokens, h_pad)

    low = (contract_rows(coords, g_all) / tokens).astype(bf16)
    back_part = contract_cols(g_all, low).astype(bf16)
    cross_part = contract_cols(low, low).astype(bf16)
    both = tokens + rank
    blk = both // (n_dp * n_ten)
    joined = jnp.concatenate([back_part, cross_part], axis=0)
    joined = joined.reshape(2, n_ten, n_z, blk, rank)
    a8 = to_blocks(acts, n_dp, w_blk)
    low8 = low.reshape(n_dp, rank_rows, h_pad)
    low_all, a_all, sums = pl.pallas_call(
        functools.partial(back_kernel, n_dp, n_ten),
        out_shape=(like(low8.shape), like(a8.shape), like(joined.shape)),
        in_specs=[ANY, ANY, VMEM],
        out_specs=(ANY, ANY, ANY),
        scratch_shapes=[
            pltpu.VMEM(joined.shape, bf16),
            pltpu.VMEM(joined.shape, bf16),
            pltpu.VMEM(joined.shape[1:], bf16),
            pltpu.VMEM(joined.shape[1:], bf16),
            pltpu.VMEM(joined.shape[2:], bf16),
            pltpu.VMEM(joined.shape[2:], bf16),
            pairs(n_dp), pairs(n_dp), pairs(2), pairs(n_ten), pairs(n_z),
            pairs(n_z), pairs(n_ten), pairs(2),
        ],
        compiler_params=params(1),
    )(low8, a8, joined)
    sums = sums.reshape(both, rank)
    back_low, cross = sums[:tokens], sums[tokens:]

    dp = lax.axis_index("dp")
    pull = contract_rows(back_low, a_all.reshape(tokens, w_blk)) / tokens
    own_cols = lax.dynamic_slice_in_dim(proj_t, dp * w_blk, w_blk, 1)
    correction = jnp.dot(cross, own_cols, preferred_element_type=jnp.float32)
    delta = (jnp.sqrt(dim) * pull - correction).astype(bf16)
    d8 = delta.reshape(n_dp, rank_rows, w_blk)
    d_all = pl.pallas_call(
        functools.partial(swap_kernel, n_dp),
        out_shape=like(d8.shape),
        in_specs=[ANY],
        out_specs=ANY,
        scratch_shapes=[pairs(n_dp)],
        compiler_params=params(2),
    )(d8)
    own_rows = lax.dynamic_slice_in_dim(proj_t, dp * rank_rows, rank_rows, 0)
    step = d_all.transpose(1, 0, 2).reshape(rank_rows, width)
    new_proj_t = own_rows.astype(jnp.float32) + step.astype(jnp.float32)

    grad_part = low_all[:, :, :h_blk].transpose(1, 0, 2).reshape(rank_rows, hidden)
    return adam(grad_part.astype(jnp.float32), first_moment, second_moment), new_proj_t


def adam(grad_part, first_moment, second_moment):
    moment_one = 0.9 * first_moment + 0.1 * grad_part
    moment_two = 0.999 * second_moment + 0.001 * grad_part * grad_part
    return moment_one / (1.0 - 0.9**10) / (jnp.sqrt(moment_two / (1.0 - 0.999**10)) + 1e-08)


def general(acts, grad_out, proj_t, first_moment, second_moment):
    tok_rows, width = acts.shape
    dim = jnp.float32(width * lax.axis_size("tensor"))
    total_tokens = tok_rows * lax.axis_size("dp")
    rank_rows = first_moment.shape[0]
    row_start = lax.axis_index("dp") * rank_rows
    local_coords = contract_cols(acts, proj_t) * (1.0 / jnp.sqrt(dim))
    coords = lax.psum(local_coords.astype(jnp.bfloat16), "tensor")
    grad_part = lax.psum_scatter(
        contract_rows(coords, grad_out) / total_tokens, "dp", scatter_dimension=0, tiled=True
    )
    low_part = grad_part.astype(jnp.bfloat16)
    piece = lax.all_gather(low_part, "dp", axis=0, tiled=True)
    back = lax.psum(contract_cols(grad_out, piece).astype(jnp.bfloat16), "tensor")
    cross = lax.psum(contract_cols(low_part, piece).astype(jnp.bfloat16), "tensor")
    pull = lax.psum_scatter(
        contract_rows(back, acts) / total_tokens, "dp", scatter_dimension=0, tiled=True
    )
    own_rows = lax.dynamic_slice_in_dim(proj_t, row_start, rank_rows, 0)
    correction = jnp.dot(
        cross.astype(jnp.float32), proj_t.astype(jnp.float32), precision=lax.Precision.HIGHEST
    )
    new_proj_t = own_rows.astype(jnp.float32) + jnp.sqrt(dim) * pull - correction
    return adam(grad_part, first_moment, second_moment), new_proj_t


def local(n_dp, n_ten, acts, grad_out, proj_t, first_moment, second_moment):
    tok_rows, width = acts.shape
    both = tok_rows * n_dp + proj_t.shape[0]
    fits = (
        n_dp % 2 == 0
        and n_dp <= 16
        and tok_rows % (16 * n_ten) == 0
        and both % (16 * n_dp * n_ten) == 0
        and first_moment.shape[0] % 16 == 0
        and width % (128 * n_dp) == 0
        and grad_out.shape[1] % n_dp == 0
    )
    args = (acts, grad_out, proj_t, first_moment, second_moment)
    return direct(n_dp, n_ten, *args) if fits else general(*args)


def solution(mesh):
    split = P("dp", "tensor")
    return jax.shard_map(
        functools.partial(local, mesh.shape["dp"], mesh.shape["tensor"]),
        mesh=mesh,
        in_specs=(split, split, P(None, "tensor"), split, split),
        out_specs=(split, split),
        check_vma=False,
    )
```

time: 296 us -> 123 us (0.42); the launches traced: 293 us -> 123 us
  waiting for transfers between devices: 255 us -> 0 us
  Pallas kernels: 0 us -> 104 us
  matrix products: 20.2 us -> 6.04 us
  between operations: 13.8 us -> 0.82 us
  local copies, waits for them, and re-layouts: 0.03 us -> 7.4 us
    reduce_scatter x2 -> x0, waiting for transfers between devices: 126 us -> none  [the longest x1 78.1 us: local(): lax.psum_scatter(contract_rows(picked, grad_out) / total_tokens, 'dp', sc...]
    pallas_call x0 -> x3, Pallas kernels: none -> 104 us  [the longest x1 50.5 us: direct(): pl.pallas_call(functools.partial(back_kernel, n_dp, n_ten), out_shape=(li...]
    psum x2 -> x0, waiting for transfers between devices: 85.3 us -> none  [the longest x1 44.6 us: local(): coords = lax.psum(local_coords.astype(jnp.bfloat16), 'tensor')]
    all_gather x1 -> x0, waiting for transfers between devices: 43.6 us -> none  [local(): piece = lax.all_gather(low_part, 'dp', axis=0, tiled=True)]
    dot_general x3, matrix products: 9.25 us -> 2.06 us  [contract_cols(): lax.dot_general(left, right, (((1,), (1,)), ((), ())), preferred_element_...]
    dot_general x2, matrix products: 8.68 us -> 2.58 us  [contract_rows(): lax.dot_general(left, right, (((0,), (0,)), ((), ())), preferred_element_...]
    unnamed x14 -> x12, local copies, waits for them, and re-layouts: 0.03 us -> 5.36 us
    convert_element_type x1, other arithmetic: 3.1 us -> 0.12 us  [direct(): grad_part.astype(jnp.float32)]
  transfers between devices with their start and end apart: 5 -> 0, of which waited for: 5 -> 0; matrix products, arithmetic and copies ran while one was open for 0% -> 0% of each run, Pallas kernels for 0% -> 0%
where the time goes in v1:
time: 123 us
  Pallas kernels  104 us (85%)
  local copies, waits for them, and re-layouts  7.4 us (6%)
  matrix products  6.04 us (5%)
  other arithmetic  4.73 us (4%)
    pallas_call x1, Pallas kernels, direct(): pl.pallas_call(functools.partial(back_kernel, n_dp, n_ten), out_shape=(li...  50.5 us
    pallas_call x1, Pallas kernels, direct(): pl.pallas_call(functools.partial(coords_kernel, n_dp, n_ten), out_shape=(...  43.8 us
    pallas_call x1, Pallas kernels, direct(): pl.pallas_call(functools.partial(swap_kernel, n_dp), out_shape=like(d8.sh...  9.5 us
    unnamed x12, local copies, waits for them, and re-layouts  5.36 us
    div x1, other arithmetic, adam(): moment_one / (1.0 - 0.9 ** 10)  2.68 us
    dot_general x2, matrix products, contract_rows(): lax.dot_general(left, right, (((0,), (0,)), ((), ())), preferred_element_...  2.58 us

profile of v1, /device:TPU:1, one launch (start us, length us, event | category | flops | bytes accessed | tf_op | source)
XLA Modules:
  0.0 122.9 jit_solution(6616630604273412110)
XLA Ops:
  0.6 1.6 %copy.7 = bf16[128,3584]{0,1:T(8,128)(2,1)S(1)} copy(bf16[128,3584]{1,0:T(8,128)(2,1)} %param.6) | data formatting | bytes 1835008 | tf_op args[1]
  2.2 0.0 copy-start.3
  2.2 0.5 copy.8
  2.7 0.0 copy-start.2
  2.8 0.2 pad.4.g8
  2.9 0.3 copy-done.3
  3.2 1.1 copy-done.2
  4.4 0.9 fusion.3
  5.2 43.8 %shard_map.68 = (bf16[8,128,512]{2,1,0:T(8,128)(2,1)S(1)}, bf16[2,4,4,32,512]{4,3,2,1,0:T(8,128)(2,1)S(1)}) custom-call(bf16[8,128,512]{2,1,0:T(8,128)(2,1)S(1)} %pad.4.g8, bf16[4,32,512]{2,1,0:T(8,128)(2,1)S(1)} %bitcast.32), custom_call_target="tpu_custom_call" | custom-call | tf_op jit(solution)/shard_map/pallas_call | solution.py:181
  49.1 0.1 copy.9
  49.2 0.7 fusion
  49.9 0.7 convolution_convert_fusion
  50.6 0.5 convolution_convert_fusion.1
  51.1 0.1 pad_maximum_fusion
  51.2 0.3 copy.10
  51.5 0.2 copy.11
  51.7 50.5 %shard_map.69 = (bf16[8,64,512]{2,1,0:T(8,128)(2,1)S(1)}, bf16[8,128,256]{2,1,0:T(8,128)(2,1)S(1)}, bf16[2,4,4,48,512]{4,3,2,1,0:T(8,128)(2,1)S(1)}) custom-call(bf16[8,64,512]{2,1,0:T(8,128)(2,1)S(1)} %bitcast.29, bf16[8,128,256]{2,1,0:T(8,128)(2,1)S(1)} %bitcast.30, bf16[2,4,4,48,512]{4,3,2,1,0:T(8,128)(2,1)S(1)} %bitcast.28), custom_call_target="tpu_custom_call" | custom-call | tf_op jit(solution)/shard_map/pallas_call | solution.py:205
  102.3 0.0 copy-start
  102.3 1.1 copy-done
  103.4 0.0 copy-start.1
  103.4 0.8 copy-done.1
  104.2 1.4 %fusion.10 = f32[512,256]{1,0:T(8,128)S(1)} fusion(bf16[1536,512]{1,0:T(8,128)(2,1)} %bitcast.34, bf16[512,2048]{1,0:T(8,128)(2,1)} %param.7, s32[]{:T(128)S(6)} %select_n.7), kind=kOutput, calls=%fused_computation.18 | convolution fusion | flops 134217728 | bytes 1310724 | tf_op jit(solution)/shard_map/dot_general | solution.py:228
  105.6 1.8 %fusion.2 = bf16[512,256]{1,0:T(8,128)(2,1)S(1)} fusion(f32[512,256]{1,0:T(8,128)S(1)} %fusion.10, bf16[1024,256]{1,0:T(8,128)(2,1)} %bitcast.38, bf16[1536,512]{1,0:T(8,128)(2,1)} %bitcast.35), kind=kOutput, calls=%fused_computation.8 | convolution fusion | flops 268828672 | bytes 2359296 | tf_op jit(solution)/shard_map/dot_general | solution.py:16
  107.5 9.5 %shard_map.70 = bf16[8,64,256]{2,1,0:T(8,128)(2,1)S(1)} custom-call(bf16[8,64,256]{2,1,0:T(8,128)(2,1)S(1)} %bitcast.33), custom_call_target="tpu_custom_call" | custom-call | tf_op jit(solution)/shard_map/pallas_call | solution.py:231
  117.1 1.8 %convert_add_fusion = f32[64,2048]{1,0:T(8,128)} fusion(f32[64,2048]{1,0:T(8,128)S(1)} %bitcast.41, bf16[512,2048]{1,0:T(8,128)(2,1)} %param.7, s32[]{:T(128)S(6)} %select_n.6), kind=kLoop, calls=%fused_computation.21 | loop fusion | flops 262144 | bytes 1310724 | tf_op jit(solution)/shard_map/add | solution.py:241
  118.9 0.1 convert_bitcast_fusion
  119.0 0.0 copy-start.4
  119.0 0.6 copy.12
  119.6 0.4 reshape.50
  120.1 0.1 copy-done.4
  120.2 2.7 %fusion.9 = f32[64,3584]{1,0:T(8,128)} fusion(f32[64,3584]{1,0:T(8,128)S(1)} %reshape.50, f32[64,3584]{1,0:T(8,128)S(1)} %copy-done.4, f32[64,3584]{1,0:T(8,128)} %param.8), kind=kLoop, calls=%fused_computation.17 | loop fusion | flops 2523136 | bytes 3670016 | tf_op jit(solution)/shard_map/div | solution.py:250
  (2 shorter events, 0.1 us)
Async XLA Ops:
  2.2 1.0 copy-start.3
  2.7 1.6 %copy-start.2 = (bf16[512,2048]{1,0:T(8,128)(2,1)S(1)}, bf16[512,2048]{1,0:T(8,128)(2,1)}, u32[]{:S(2)}) copy-start(bf16[512,2048]{1,0:T(8,128)(2,1)} %param.7) | copy-start | bytes 6291460
  102.3 1.2 copy-start
  103.4 0.8 copy-start.1
  119.0 1.2 copy-start.4

commit v2 on v1

--- a/solution.py
+++ b/solution.py
@@ -10,6 +10,7 @@
 MESH = pl.DeviceIdType.MESH
 ANY = pl.BlockSpec(memory_space=pl.ANY)
 VMEM = pl.BlockSpec(memory_space=pltpu.VMEM)
+PARTS = 3
 
 
 def contract_rows(left, right):
@@ -56,15 +57,20 @@
     return copy
 
 
-def start_swap(src, dst, sems, n_dp):
+def start_swap(src, dst, sems, n_dp, steps=None):
     dp, _, _, ten = place()
     copies = []
-    for k in range(1, n_dp):
+    for k in steps or range(1, n_dp):
         peer = lax.rem(dp + k, n_dp)
         copies.append(send(src.at[peer], dst.at[dp], sems, k, (peer, ten)))
+    return copies
+
+
+def start_own(src, dst, sems):
+    dp = place()[0]
     own = pltpu.make_async_copy(src.at[dp], dst.at[dp], sems.at[0, 0])
     own.start()
-    return copies + [own]
+    return [own]
 
 
 def wait_all(copies):
@@ -72,44 +78,60 @@
         copy.wait()
 
 
-def reduce_stage(src, got, sems, me, n, device):
+def start_reduce(src, got, sems, base, me, n, device):
     copies = []
     for k in range(1, n):
         peer = lax.rem(me + k, n)
-        copies.append(send(src.at[peer], got.at[k], sems, k, device(peer)))
+        copies.append(send(src.at[peer], got.at[k], sems, base + k, device(peer)))
+    return copies
+
+
+def end_reduce(copies, src, got, me):
     total = src[me].astype(jnp.float32)
-    for k in range(1, n):
-        copies[k - 1].wait()
+    for k, copy in enumerate(copies, 1):
+        copy.wait()
         total = total + got[k].astype(jnp.float32)
     return total
 
 
-def gather_stages(full, sems_z, sems_t, sems_c, n_z, n_ten):
+def gather_stages(full, sems, base, n_z, n_ten):
     _, z, c, ten = place()
     copies = []
     mine = full.at[c, ten, z]
     for k in range(1, n_z):
         peer = lax.rem(z + k, n_z)
-        copies.append(send(mine, mine, sems_z, k, (peer * 2 + c, ten)))
+        copies.append(send(mine, mine, sems[0], base * n_z + k, (peer * 2 + c, ten)))
+    yield
     wait_all(copies)
     copies = []
     mine = full.at[c, ten]
     for k in range(1, n_ten):
         peer = lax.rem(ten + k, n_ten)
-        copies.append(send(mine, mine, sems_t, k, (z * 2 + c, peer)))
+        copies.append(send(mine, mine, sems[1], base * n_ten + k, (z * 2 + c, peer)))
+    yield
     wait_all(copies)
     mine = full.at[c]
-    send(mine, mine, sems_c, 1, (z * 2 + 1 - c, ten)).wait()
+    copy = send(mine, mine, sems[2], base * 2 + 1, (z * 2 + 1 - c, ten))
+    yield
+    copy.wait()
 
 
 def coords_kernel(n_dp, n_ten, g8, part, g_all, full_out, full, got, s_g, s_r, s_z, s_t, s_c):
     n_z = n_dp // 2
     dp, z, c, ten = place()
+    near = [k for k in range(1, n_dp) if k < 3 or k > n_dp - 3]
+    far = [k for k in range(1, n_dp) if k not in near]
     greet(n_dp, n_ten)
-    total = reduce_stage(part, got, s_r, ten, n_ten, lambda p: (dp, p))
-    swaps = start_swap(g8, g_all, s_g, n_dp)
-    full[c, ten, z] = total.astype(full.dtype)
-    gather_stages(full, s_z, s_t, s_c, n_z, n_ten)
+    copies = start_reduce(part, got, s_r, 0, ten, n_ten, lambda p: (dp, p))
+    swaps = start_swap(g8, g_all, s_g, n_dp, near) + start_own(g8, g_all, s_g)
+    full[c, ten, z] = end_reduce(copies, part, got, ten).astype(full.dtype)
+    stages = gather_stages(full, (s_z, s_t, s_c), 0, n_z, n_ten)
+    next(stages)
+    next(stages)
+    if far:
+        swaps += start_swap(g8, g_all, s_g, n_dp, far)
+    for _ in stages:
+        pass
     out = pltpu.make_async_copy(full, full_out, s_c.at[0, 0])
     out.start()
     wait_all(swaps + [out])
@@ -121,17 +143,39 @@
 ):
     n_z = n_dp // 2
     dp, z, c, ten = place()
+    parts = part.shape[0]
+
+    def stages(p):
+        copies = start_reduce(
+            part.at[p], got_c.at[p], s_rc, p * 2, c, 2, lambda q: (z * 2 + q, ten)
+        )
+        yield
+        mid_c[p] = end_reduce(copies, part.at[p], got_c.at[p], c).astype(mid_c.dtype)
+        copies = start_reduce(
+            mid_c.at[p], got_t.at[p], s_rt, p * n_ten, ten, n_ten, lambda q: (dp, q)
+        )
+        yield
+        mid_t[p] = end_reduce(copies, mid_c.at[p], got_t.at[p], ten).astype(mid_t.dtype)
+        copies = start_reduce(
+            mid_t.at[p], got_z.at[p], s_rz, p * n_z, z, n_z, lambda q: (q * 2 + c, ten)
+        )
+        yield
+        total = end_reduce(copies, mid_t.at[p], got_z.at[p], z)
+        full[p, c, ten, z] = total.astype(full.dtype)
+        yield from gather_stages(full.at[p], (s_z, s_t, s_c), p, n_z, n_ten)
+
     greet(n_dp, n_ten)
-    mid_c[...] = reduce_stage(
-        part, got_c, s_rc, c, 2, lambda p: (z * 2 + p, ten)
-    ).astype(mid_c.dtype)
-    swaps = start_swap(low8, low_all, s_l, n_dp) + start_swap(a8, a_all, s_a, n_dp)
-    mid_t[...] = reduce_stage(
-        mid_c, got_t, s_rt, ten, n_ten, lambda p: (dp, p)
-    ).astype(mid_t.dtype)
-    total = reduce_stage(mid_t, got_z, s_rz, z, n_z, lambda p: (p * 2 + c, ten))
-    full[c, ten, z] = total.astype(full.dtype)
-    gather_stages(full, s_z, s_t, s_c, n_z, n_ten)
+    chains = [stages(p) for p in range(parts)]
+    for chain in chains:
+        next(chain)
+    swaps = start_swap(low8, low_all, s_l, n_dp) + start_own(low8, low_all, s_l)
+    swaps += start_own(a8, a_all, s_a)
+    for when in range(1, 6 + parts):
+        for p in reversed(range(parts)):
+            if 1 <= when - p <= 6:
+                next(chains[p], None)
+                if p == parts - 1 and when - p == 4:
+                    swaps += start_swap(a8, a_all, s_a, n_dp)
     out = pltpu.make_async_copy(full, full_out, s_c.at[0, 0])
     out.start()
     wait_all(swaps + [out])
@@ -139,7 +183,7 @@
 
 def swap_kernel(n_dp, src, dst, sems):
     greet(n_dp, 1)
-    wait_all(start_swap(src, dst, sems, n_dp))
+    wait_all(start_swap(src, dst, sems, n_dp) + start_own(src, dst, sems))
 
 
 def pairs(n):
@@ -199,7 +243,8 @@
     both = tokens + rank
     blk = both // (n_dp * n_ten)
     joined = jnp.concatenate([back_part, cross_part], axis=0)
-    joined = joined.reshape(2, n_ten, n_z, blk, rank)
+    parts = PARTS if blk % (16 * PARTS) == 0 else 1
+    joined = joined.reshape(parts, 2, n_ten, n_z, blk // parts, rank)
     a8 = to_blocks(acts, n_dp, w_blk)
     low8 = low.reshape(n_dp, rank_rows, h_pad)
     low_all, a_all, sums = pl.pallas_call(
@@ -210,12 +255,12 @@
         scratch_shapes=[
             pltpu.VMEM(joined.shape, bf16),
             pltpu.VMEM(joined.shape, bf16),
-            pltpu.VMEM(joined.shape[1:], bf16),
-            pltpu.VMEM(joined.shape[1:], bf16),
-            pltpu.VMEM(joined.shape[2:], bf16),
-            pltpu.VMEM(joined.shape[2:], bf16),
-            pairs(n_dp), pairs(n_dp), pairs(2), pairs(n_ten), pairs(n_z),
-            pairs(n_z), pairs(n_ten), pairs(2),
+            pltpu.VMEM((parts,) + joined.shape[2:], bf16),
+            pltpu.VMEM((parts,) + joined.shape[2:], bf16),
+            pltpu.VMEM((parts,) + joined.shape[3:], bf16),
+            pltpu.VMEM((parts,) + joined.shape[3:], bf16),
+            pairs(n_dp), pairs(n_dp), pairs(parts * 2), pairs(parts * n_ten), pairs(parts * n_z),
+            pairs(parts * n_z), pairs(parts * n_ten), pairs(parts * 2),
         ],
         compiler_params=params(1),
     )(low8, a8, joined)

time: 123 us -> 96.8 us (0.79)
  Pallas kernels: 104 us -> 78.2 us
  matrix products: 6.04 us -> 4.58 us
    pallas_call x1, Pallas kernels: 50.5 us -> 36 us  [direct(): pl.pallas_call(functools.partial(back_kernel, n_dp, n_ten), out_shape=(li...]
    pallas_call x1, Pallas kernels: 43.8 us -> 32.9 us  [direct(): pl.pallas_call(functools.partial(coords_kernel, n_dp, n_ten), out_shape=(...]
    dot_general x2, matrix products: 2.58 us -> 1.22 us  [contract_rows(): lax.dot_general(left, right, (((0,), (0,)), ((), ())), preferred_element_...]
    slice x0 -> x2, local copies, waits for them, and re-layouts: none -> 1.36 us  [direct(): back_low, cross = (sums[:tokens], sums[tokens:])]
    unnamed x12 -> x14, local copies, waits for them, and re-layouts: 5.36 us -> 4.67 us
where the time goes in v2:
time: 96.8 us; the launch traced here: 96.4 us
  Pallas kernels  78.2 us (81%)
  local copies, waits for them, and re-layouts  8.07 us (8%)
  other arithmetic  4.73 us (5%)
  matrix products  4.58 us (5%)
    pallas_call x1, Pallas kernels, direct(): pl.pallas_call(functools.partial(back_kernel, n_dp, n_ten), out_shape=(li...  36 us
    pallas_call x1, Pallas kernels, direct(): pl.pallas_call(functools.partial(coords_kernel, n_dp, n_ten), out_shape=(...  32.9 us
    pallas_call x1, Pallas kernels, direct(): pl.pallas_call(functools.partial(swap_kernel, n_dp), out_shape=like(d8.sh...  9.23 us
    unnamed x14, local copies, waits for them, and re-layouts  4.67 us
    div x1, other arithmetic, adam(): moment_one / (1.0 - 0.9 ** 10)  2.68 us
    dot_general x3, matrix products, contract_cols(): lax.dot_general(left, right, (((1,), (1,)), ((), ())), preferred_element_...  2.07 us

profile of v2, /device:TPU:1, one launch (start us, length us, event | category | flops | bytes accessed | tf_op | source)
XLA Modules:
  0.0 96.4 jit_solution(2150142761609825620)
XLA Ops:
  0.6 1.6 %copy.7 = bf16[128,3584]{0,1:T(8,128)(2,1)S(1)} copy(bf16[128,3584]{1,0:T(8,128)(2,1)} %param.6) | data formatting | bytes 1835008 | tf_op args[1]
  2.2 0.0 copy-start.4
  2.2 0.5 copy.8
  2.7 0.0 copy-start.3
  2.8 0.2 pad.4.g8
  2.9 0.3 copy-done.4
  3.2 1.1 %copy-done.3 = bf16[512,2048]{1,0:T(8,128)(2,1)S(1)} copy-done((bf16[512,2048]{1,0:T(8,128)(2,1)S(1)}, bf16[512,2048]{1,0:T(8,128)(2,1)}, u32[]{:S(2)}) %copy-start.3) | copy-done | bytes 2097176
  4.4 0.9 fusion.3
  5.2 32.9 %shard_map.68 = (bf16[8,128,512]{2,1,0:T(8,128)(2,1)S(1)}, bf16[2,4,4,32,512]{4,3,2,1,0:T(8,128)(2,1)S(1)}) custom-call(bf16[8,128,512]{2,1,0:T(8,128)(2,1)S(1)} %pad.4.g8, bf16[4,32,512]{2,1,0:T(8,128)(2,1)S(1)} %bitcast.35), custom_call_target="tpu_custom_call" | custom-call | tf_op jit(solution)/shard_map/pallas_call | solution.py:225
  38.2 0.1 copy.9
  38.3 0.7 fusion
  39.0 0.7 convolution_convert_fusion
  39.8 0.5 convolution_convert_fusion.1
  40.2 0.1 pad_maximum_fusion
  40.3 0.3 copy.10
  40.6 0.2 copy.11
  40.8 36.0 %shard_map.69 = (bf16[8,64,512]{2,1,0:T(8,128)(2,1)S(1)}, bf16[8,128,256]{2,1,0:T(8,128)(2,1)S(1)}, bf16[3,2,4,4,16,512]{5,4,3,2,1,0:T(8,128)(2,1)S(1)}) custom-call(bf16[8,64,512]{2,1,0:T(8,128)(2,1)S(1)} %bitcast.32, bf16[8,128,256]{2,1,0:T(8,128)(2,1)S(1)} %bitcast.33, bf16[3,2,4,4,16,512]{5,4,3,2,1,0:T(8,128)(2,1)S(1)} %bitcast.31), custom_call_target="tpu_custom_call" | custom-call | tf_op jit(solution)/shard_map/pallas_call | solution.py:250
  76.9 0.0 copy-start
  76.9 0.0 copy-start.1
  76.9 1.1 %copy-done = bf16[3,2,4,4,16,512]{5,4,3,2,1,0:T(8,128)(2,1)} copy-done((bf16[3,2,4,4,16,512]{5,4,3,2,1,0:T(8,128)(2,1)}, bf16[3,2,4,4,16,512]{5,4,3,2,1,0:T(8,128)(2,1)S(1)}, u32[]{:S(2)}) %copy-start) | copy-done | bytes 1572888
  78.1 0.1 copy-done.1
  78.2 1.3 %fusion.9 = f32[512,256]{1,0:T(8,128)S(1)} fusion(bf16[512,512]{1,0:T(8,128)(2,1)S(1)} %bitcast.42, bf16[512,2048]{1,0:T(8,128)(2,1)} %param.7, s32[]{:T(128)S(6)} %select_n.7), kind=kOutput, calls=%fused_computation.19 | convolution fusion | flops 134217728 | bytes 1310724 | tf_op jit(solution)/shard_map/dot_general | solution.py:273
  79.5 1.3 %slice.16 = bf16[2,2,4,4,16,512]{5,4,3,2,1,0:T(8,128)(2,1)S(1)} slice(bf16[3,2,4,4,16,512]{5,4,3,2,1,0:T(8,128)(2,1)} %copy-done), slice={[0:2], [0:2], [0:4], [0:4], [0:16], [0:512]} | slice | bytes 2097152 | tf_op jit(solution)/shard_map/slice | solution.py:268
  80.8 0.5 fusion.2
  81.3 9.2 %shard_map.70 = bf16[8,64,256]{2,1,0:T(8,128)(2,1)S(1)} custom-call(bf16[8,64,256]{2,1,0:T(8,128)(2,1)S(1)} %bitcast.36), custom_call_target="tpu_custom_call" | custom-call | tf_op jit(solution)/shard_map/pallas_call | solution.py:276
  90.6 1.8 %convert_add_fusion = f32[64,2048]{1,0:T(8,128)} fusion(f32[64,2048]{1,0:T(8,128)S(1)} %bitcast.43, bf16[512,2048]{1,0:T(8,128)(2,1)} %param.7, s32[]{:T(128)S(6)} %select_n.6), kind=kLoop, calls=%fused_computation.18 | loop fusion | flops 262144 | bytes 1310724 | tf_op jit(solution)/shard_map/add | solution.py:286
  92.4 0.1 convert_bitcast_fusion
  92.6 0.0 copy-start.5
  92.6 0.6 copy.12
  93.2 0.4 reshape.49
  93.6 0.1 copy-done.5
  93.7 2.7 %fusion.8 = f32[64,3584]{1,0:T(8,128)} fusion(f32[64,3584]{1,0:T(8,128)S(1)} %reshape.49, f32[64,3584]{1,0:T(8,128)S(1)} %copy-done.5, f32[64,3584]{1,0:T(8,128)} %param.8), kind=kLoop, calls=%fused_computation.16 | loop fusion | flops 2523136 | bytes 3670016 | tf_op jit(solution)/shard_map/div | solution.py:295
  (5 shorter events, 0.1 us)
Async XLA Ops:
  2.2 1.0 %copy-start.4 = (bf16[128,2048]{1,0:T(8,128)(2,1)S(1)}, bf16[128,2048]{1,0:T(8,128)(2,1)}, u32[]{:S(2)}) copy-start(bf16[128,2048]{1,0:T(8,128)(2,1)} %param.5) | copy-start | bytes 1572868
  2.7 1.6 %copy-start.3 = (bf16[512,2048]{1,0:T(8,128)(2,1)S(1)}, bf16[512,2048]{1,0:T(8,128)(2,1)}, u32[]{:S(2)}) copy-start(bf16[512,2048]{1,0:T(8,128)(2,1)} %param.7) | copy-start | bytes 6291460
  76.9 1.1 %copy-start = (bf16[3,2,4,4,16,512]{5,4,3,2,1,0:T(8,128)(2,1)}, bf16[3,2,4,4,16,512]{5,4,3,2,1,0:T(8,128)(2,1)S(1)}, u32[]{:S(2)}) copy-start(bf16[3,2,4,4,16,512]{5,4,3,2,1,0:T(8,128)(2,1)S(1)} %get-tuple-element.10) | copy-start | bytes 4718596
  76.9 1.3 %copy-start.1 = (bf16[8,128,256]{2,1,0:T(8,128)(2,1)}, bf16[8,128,256]{2,1,0:T(8,128)(2,1)S(1)}, u32[]{:S(2)}) copy-start(bf16[8,128,256]{2,1,0:T(8,128)(2,1)S(1)} %get-tuple-element.11) | copy-start | bytes 1572868
  78.2 2.6 %copy-start.2 = (bf16[8,128,256]{2,1,0:T(8,128)(2,1)S(1)}, bf16[8,128,256]{2,1,0:T(8,128)(2,1)}, u32[]{:S(2)}) copy-start(bf16[8,128,256]{2,1,0:T(8,128)(2,1)} %copy-done.1) | copy-start | bytes 1572868
  92.6 1.2 %copy-start.5 = (f32[64,3584]{1,0:T(8,128)S(1)}, f32[64,3584]{1,0:T(8,128)}, u32[]{:S(2)}) copy-start(f32[64,3584]{1,0:T(8,128)} %param.9) | copy-start | bytes 2752516

commit v3 on v2

--- a/solution.py
+++ b/solution.py
@@ -62,15 +62,20 @@
     copies = []
     for k in steps or range(1, n_dp):
         peer = lax.rem(dp + k, n_dp)
-        copies.append(send(src.at[peer], dst.at[dp], sems, k, (peer, ten)))
+        copies.append(send(src(peer), dst.at[dp], sems, k, (peer, ten)))
     return copies
 
 
 def start_own(src, dst, sems):
     dp = place()[0]
-    own = pltpu.make_async_copy(src.at[dp], dst.at[dp], sems.at[0, 0])
+    own = pltpu.make_async_copy(src(dp), dst.at[dp], sems.at[0, 0])
     own.start()
     return [own]
+
+
+def columns(ref, n, span):
+    block = ref.shape[1] // n
+    return lambda p: ref.at[:, pl.ds(pl.multiple_of(lax.div(p * block, 128) * 128, 128), span)]
 
 
 def wait_all(copies):
@@ -116,9 +121,10 @@
     copy.wait()
 
 
-def coords_kernel(n_dp, n_ten, g8, part, g_all, full_out, full, got, s_g, s_r, s_z, s_t, s_c):
+def coords_kernel(n_dp, n_ten, grad_out, part, g_all, full_out, full, got, s_g, s_r, s_z, s_t, s_c):
     n_z = n_dp // 2
     dp, z, c, ten = place()
+    g8 = columns(grad_out, n_dp, g_all.shape[2])
     near = [k for k in range(1, n_dp) if k < 3 or k > n_dp - 3]
     far = [k for k in range(1, n_dp) if k not in near]
     greet(n_dp, n_ten)
@@ -138,12 +144,14 @@
 
 
 def back_kernel(
-    n_dp, n_ten, low8, a8, part, low_all, a_all, full_out,
+    n_dp, n_ten, low, acts, part, low_all, a_all, full_out,
     full, got_c, mid_c, got_t, mid_t, got_z, s_l, s_a, s_rc, s_rt, s_rz, s_z, s_t, s_c,
 ):
     n_z = n_dp // 2
     dp, z, c, ten = place()
     parts = part.shape[0]
+    low8 = lambda p: low.at[p]
+    a8 = columns(acts, n_dp, a_all.shape[2])
 
     def stages(p):
         copies = start_reduce(
@@ -181,9 +189,27 @@
     wait_all(swaps + [out])
 
 
-def swap_kernel(n_dp, src, dst, sems):
+def finish_kernel(
+    n_dp, d8, low_all, first_moment, second_moment, own_rows, adam_step, new_proj_t, got, sems
+):
+    block = got.shape[2]
+    hidden, span = adam_step.shape[1], low_all.shape[2]
     greet(n_dp, 1)
-    wait_all(start_swap(src, dst, sems, n_dp) + start_own(src, dst, sems))
+    copies = start_swap(lambda p: d8.at[p], got, sems, n_dp)
+    copies += start_own(lambda p: d8.at[p], got, sems)
+    for lo in range(0, hidden, 128):
+        grad = 0.0
+        for p in range(n_dp):
+            start, stop = p * hidden // n_dp, (p + 1) * hidden // n_dp
+            if start < lo + 128 and stop > lo:
+                at = lo - start // 128 * 128
+                grad = grad + low_all[p, :, at:at + 128].astype(jnp.float32)
+        cols = slice(lo, lo + 128)
+        adam_step[:, cols] = adam(grad, first_moment[:, cols], second_moment[:, cols])
+    wait_all(copies)
+    for p in range(n_dp):
+        cols = slice(p * block, (p + 1) * block)
+        new_proj_t[:, cols] = own_rows[:, cols].astype(jnp.float32) + got[p].astype(jnp.float32)
 
 
 def pairs(n):
@@ -200,10 +226,9 @@
     return jax.ShapeDtypeStruct(shape, dtype)
 
 
-def to_blocks(x, n, width):
-    rows, cols = x.shape
-    x = x.reshape(rows, n, cols // n).transpose(1, 0, 2)
-    return jnp.pad(x, ((0, 0), (0, 0), (0, width - cols // n)))
+def span_of(cols, n):
+    block = cols // n
+    return max(-(-(p * block % 128 + block) // 128) * 128 for p in range(n))
 
 
 def direct(n_dp, n_ten, acts, grad_out, proj_t, first_moment, second_moment):
@@ -216,15 +241,14 @@
     dim = jnp.float32(width * n_ten)
     bf16 = jnp.bfloat16
     h_blk = hidden // n_dp
-    h_pad = -(-h_blk // 128) * 128
+    h_pad = span_of(hidden, n_dp)
     w_blk = width // n_dp
     sub = tok_rows // n_ten
 
     part = (contract_cols(acts, proj_t) * (1.0 / jnp.sqrt(dim))).astype(bf16)
-    g8 = to_blocks(grad_out, n_dp, h_pad)
     g_all, coords = pl.pallas_call(
         functools.partial(coords_kernel, n_dp, n_ten),
-        out_shape=(like(g8.shape), like((2, n_ten, n_z, sub, rank))),
+        out_shape=(like((n_dp, tok_rows, h_pad)), like((2, n_ten, n_z, sub, rank))),
         in_specs=[ANY, VMEM],
         out_specs=(ANY, ANY),
         scratch_shapes=[
@@ -233,11 +257,14 @@
             pairs(n_dp), pairs(n_ten), pairs(n_z), pairs(n_ten), pairs(2),
         ],
         compiler_params=params(0),
-    )(g8, part.reshape(n_ten, sub, rank))
+    )(grad_out, part.reshape(n_ten, sub, rank))
     coords = coords.transpose(2, 0, 1, 3, 4).reshape(tokens, rank)
     g_all = g_all.reshape(tokens, h_pad)
 
-    low = (contract_rows(coords, g_all) / tokens).astype(bf16)
+    dp = lax.axis_index("dp")
+    place_in = lax.broadcasted_iota(jnp.int32, (1, h_pad), 1) - lax.rem(dp * h_blk, 128)
+    low = contract_rows(coords, g_all) / tokens
+    low = jnp.where((place_in >= 0) & (place_in < h_blk), low, 0.0).astype(bf16)
     back_part = contract_cols(g_all, low).astype(bf16)
     cross_part = contract_cols(low, low).astype(bf16)
     both = tokens + rank
@@ -245,11 +272,10 @@
     joined = jnp.concatenate([back_part, cross_part], axis=0)
     parts = PARTS if blk % (16 * PARTS) == 0 else 1
     joined = joined.reshape(parts, 2, n_ten, n_z, blk // parts, rank)
-    a8 = to_blocks(acts, n_dp, w_blk)
     low8 = low.reshape(n_dp, rank_rows, h_pad)
     low_all, a_all, sums = pl.pallas_call(
         functools.partial(back_kernel, n_dp, n_ten),
-        out_shape=(like(low8.shape), like(a8.shape), like(joined.shape)),
+        out_shape=(like(low8.shape), like((n_dp, tok_rows, w_blk)), like(joined.shape)),
         in_specs=[ANY, ANY, VMEM],
         out_specs=(ANY, ANY, ANY),
         scratch_shapes=[
@@ -263,30 +289,26 @@
             pairs(parts * n_z), pairs(parts * n_ten), pairs(parts * 2),
         ],
         compiler_params=params(1),
-    )(low8, a8, joined)
+    )(low8, acts, joined)
     sums = sums.reshape(both, rank)
     back_low, cross = sums[:tokens], sums[tokens:]
 
-    dp = lax.axis_index("dp")
     pull = contract_rows(back_low, a_all.reshape(tokens, w_blk)) / tokens
     own_cols = lax.dynamic_slice_in_dim(proj_t, dp * w_blk, w_blk, 1)
     correction = jnp.dot(cross, own_cols, preferred_element_type=jnp.float32)
     delta = (jnp.sqrt(dim) * pull - correction).astype(bf16)
     d8 = delta.reshape(n_dp, rank_rows, w_blk)
-    d_all = pl.pallas_call(
-        functools.partial(swap_kernel, n_dp),
-        out_shape=like(d8.shape),
-        in_specs=[ANY],
-        out_specs=ANY,
-        scratch_shapes=[pairs(n_dp)],
+    own_rows = lax.dynamic_slice_in_dim(proj_t, dp * rank_rows, rank_rows, 0)
+    return pl.pallas_call(
+        functools.partial(finish_kernel, n_dp),
+        out_shape=(
+            like((rank_rows, hidden), jnp.float32), like((rank_rows, width), jnp.float32)
+        ),
+        in_specs=[ANY, VMEM, VMEM, VMEM, VMEM],
+        out_specs=(VMEM, VMEM),
+        scratch_shapes=[pltpu.VMEM(d8.shape, bf16), pairs(n_dp)],
         compiler_params=params(2),
-    )(d8)
-    own_rows = lax.dynamic_slice_in_dim(proj_t, dp * rank_rows, rank_rows, 0)
-    step = d_all.transpose(1, 0, 2).reshape(rank_rows, width)
-    new_proj_t = own_rows.astype(jnp.float32) + step.astype(jnp.float32)
-
-    grad_part = low_all[:, :, :h_blk].transpose(1, 0, 2).reshape(rank_rows, hidden)
-    return adam(grad_part.astype(jnp.float32), first_moment, second_moment), new_proj_t
+    )(d8, low_all, first_moment, second_moment, own_rows)
 
 
 def adam(grad_part, first_moment, second_moment):
@@ -331,7 +353,7 @@
         and both % (16 * n_dp * n_ten) == 0
         and first_moment.shape[0] % 16 == 0
         and width % (128 * n_dp) == 0
-        and grad_out.shape[1] % n_dp == 0
+        and grad_out.shape[1] % (128 * (n_dp // 2)) == 0
     )
     args = (acts, grad_out, proj_t, first_moment, second_moment)
     return direct(n_dp, n_ten, *args) if fits else general(*args)

time: 96.8 us -> 93.2 us (0.963)
  other arithmetic: 4.73 us -> 0.11 us
    div x1 -> x0, other arithmetic: 2.68 us -> none  [adam(): moment_one / (1.0 - 0.9 ** 10)]
    unnamed x14 -> x20, local copies, waits for them, and re-layouts: 4.67 us -> 7.11 us
    add x1 -> x0, other arithmetic: 1.79 us -> none  [direct(): new_proj_t = own_rows.astype(jnp.float32) + step.astype(jnp.float32)]
    convert_element_type x3 -> x0, local copies, waits for them, and re-layouts: 1.06 us -> none  [the longest x2 1.02 us: direct(): grad_part.astype(jnp.float32)]
    dot_general x3, matrix products: 2.07 us -> 3.08 us  [contract_cols(): lax.dot_general(left, right, (((1,), (1,)), ((), ())), preferred_element_...]
    dot_general x1, matrix products: 1.3 us -> 0.31 us  [direct(): correction = jnp.dot(cross, own_cols, preferred_element_type=jnp.float32)]
where the time goes in v3:
time: 93.2 us; the launch traced here: 92.9 us
  Pallas kernels  78.1 us (84%)
  local copies, waits for them, and re-layouts  8.56 us (9%)
  matrix products  5.31 us (6%)
    pallas_call x1, Pallas kernels, direct(): pl.pallas_call(functools.partial(back_kernel, n_dp, n_ten), out_shape=(li...  36 us
    pallas_call x1, Pallas kernels, direct(): pl.pallas_call(functools.partial(coords_kernel, n_dp, n_ten), out_shape=(...  32.9 us
    pallas_call x1, Pallas kernels, direct(): pl.pallas_call(functools.partial(finish_kernel, n_dp), out_shape=(like((r...  9.18 us
    unnamed x20, local copies, waits for them, and re-layouts  7.11 us
    dot_general x3, matrix products, contract_cols(): lax.dot_general(left, right, (((1,), (1,)), ((), ())), preferred_element_...  3.08 us
    dot_general x2, matrix products, contract_rows(): lax.dot_general(left, right, (((0,), (0,)), ((), ())), preferred_element_...  1.92 us

profile of v3, /device:TPU:1, one launch (start us, length us, event | category | flops | bytes accessed | tf_op | source)
XLA Modules:
  0.0 92.9 jit_solution(11905160798029087150)
XLA Ops:
  0.6 0.0 copy-start
  0.6 0.0 copy-start.3
  0.7 1.6 %copy-done = bf16[512,2048]{1,0:T(8,128)(2,1)S(1)} copy-done((bf16[512,2048]{1,0:T(8,128)(2,1)S(1)}, bf16[512,2048]{1,0:T(8,128)(2,1)}, u32[]{:S(2)}) %copy-start) | copy-done | bytes 2097176
  2.2 1.9 %fusion.4 = bf16[128,512]{1,0:T(8,128)(2,1)S(1)} fusion(bf16[128,2048]{1,0:T(8,128)(2,1)} %acts.1, bf16[512,2048]{1,0:T(8,128)(2,1)S(1)} %copy-done), kind=kOutput, calls=%fused_computation.10 | convolution fusion | flops 268566528 | bytes 2752512 | tf_op jit(solution)/shard_map/dot_general | solution.py:23
  4.1 0.0 copy-done.3
  4.1 32.9 %shard_map.68 = (bf16[8,128,512]{2,1,0:T(8,128)(2,1)S(1)}, bf16[2,4,4,32,512]{4,3,2,1,0:T(8,128)(2,1)S(1)}) custom-call(bf16[128,3584]{1,0:T(8,128)(2,1)S(1)} %copy-done.3, bf16[4,32,512]{2,1,0:T(8,128)(2,1)S(1)} %bitcast.24), custom_call_target="tpu_custom_call" | custom-call | tf_op jit(solution)/shard_map/pallas_call | solution.py:249
  37.1 0.1 copy.7
  37.1 0.7 fusion.1
  37.9 0.7 convolution_convert_fusion
  38.6 0.0 copy-start.1
  38.6 0.5 convolution_convert_fusion.1
  39.1 0.1 pad_maximum_fusion
  39.2 0.4 copy-done.1
  39.7 36.0 %shard_map.69 = (bf16[8,64,512]{2,1,0:T(8,128)(2,1)S(1)}, bf16[8,128,256]{2,1,0:T(8,128)(2,1)S(1)}, bf16[3,2,4,4,16,512]{5,4,3,2,1,0:T(8,128)(2,1)S(1)}) custom-call(bf16[8,64,512]{2,1,0:T(8,128)(2,1)S(1)} %bitcast.22, bf16[128,2048]{1,0:T(8,128)(2,1)S(1)} %copy-done.1, bf16[3,2,4,4,16,512]{5,4,3,2,1,0:T(8,128)(2,1)S(1)} %bitcast.21), custom_call_target="tpu_custom_call" | custom-call | tf_op jit(solution)/shard_map/pallas_call | solution.py:276
  75.7 0.0 copy-start.2
  75.7 0.0 copy-start.7
  75.7 1.1 %copy-done.2 = bf16[3,2,4,4,16,512]{5,4,3,2,1,0:T(8,128)(2,1)} copy-done((bf16[3,2,4,4,16,512]{5,4,3,2,1,0:T(8,128)(2,1)}, bf16[3,2,4,4,16,512]{5,4,3,2,1,0:T(8,128)(2,1)S(1)}, u32[]{:S(2)}) %copy-start.2) | copy-done | bytes 1572888
  76.9 0.1 copy-done.7
  77.0 0.0 copy-start.8
  77.0 0.3 fusion.5
  77.3 1.3 %slice.12 = bf16[2,2,4,4,16,512]{5,4,3,2,1,0:T(8,128)(2,1)S(1)} slice(bf16[3,2,4,4,16,512]{5,4,3,2,1,0:T(8,128)(2,1)} %copy-done.2), slice={[0:2], [0:2], [0:4], [0:4], [0:16], [0:512]} | slice | bytes 2097152 | tf_op jit(solution)/shard_map/slice | solution.py:294
  78.6 0.0 copy-start.4
  78.6 0.0 copy-done.8
  78.6 1.2 %fusion.3 = bf16[512,256]{1,0:T(8,128)(2,1)} fusion(f32[512,256]{1,0:T(8,128)S(1)} %fusion.5, bf16[1024,512]{1,0:T(8,128)(2,1)S(1)} %bitcast.30, bf16[1024,256]{1,0:T(8,128)(2,1)S(1)} %bitcast.28), kind=kOutput, calls=%fused_computation.8 | convolution fusion | flops 268828672 | bytes 2359296 | tf_op jit(solution)/shard_map/dot_general | solution.py:17
  79.8 0.0 copy-done.4
  79.9 0.0 copy-start.5
  79.9 1.2 %copy-done.5 = f32[64,3584]{1,0:T(8,128)S(1)} copy-done((f32[64,3584]{1,0:T(8,128)S(1)}, f32[64,3584]{1,0:T(8,128)}, u32[]{:S(2)}) %copy-start.5) | copy-done | bytes 917528
  81.0 0.0 copy-start.6
  81.0 0.9 %copy-done.6 = bf16[512,256]{1,0:T(8,128)(2,1)S(1)} copy-done((bf16[512,256]{1,0:T(8,128)(2,1)S(1)}, bf16[512,256]{1,0:T(8,128)(2,1)}, u32[]{:S(2)}) %copy-start.6) | copy-done | bytes 262168
  82.0 9.2 %shard_map.70 = (f32[64,3584]{1,0:T(8,128)S(1)}, f32[64,2048]{1,0:T(8,128)S(1)}) custom-call(bf16[8,64,256]{2,1,0:T(8,128)(2,1)S(1)} %bitcast.25, bf16[8,64,512]{2,1,0:T(8,128)(2,1)S(1)} %get-tuple-element.11.low_all, f32[64,3584]{1,0:T(8,128)S(1)} %copy-done.4, f32[64,3584]{1,0:T(8,128)S(1)} %copy-done.5, ...), custom_call_target="tpu_custom_call" | custom-call | tf_op jit(solution)/shard_map/pallas_call | solution.py:302
  91.2 0.9 copy.10
  92.1 0.8 copy.11
  (3 shorter events, 0.1 us)
Async XLA Ops:
  0.6 1.6 %copy-start = (bf16[512,2048]{1,0:T(8,128)(2,1)S(1)}, bf16[512,2048]{1,0:T(8,128)(2,1)}, u32[]{:S(2)}) copy-start(bf16[512,2048]{1,0:T(8,128)(2,1)} %param.7) | copy-start | bytes 6291460
  0.6 3.5 %copy-start.3 = (bf16[128,3584]{1,0:T(8,128)(2,1)S(1)}, bf16[128,3584]{1,0:T(8,128)(2,1)}, u32[]{:S(2)}) copy-start(bf16[128,3584]{1,0:T(8,128)(2,1)} %grad_out.1) | copy-start | bytes 2752516
  38.6 1.0 %copy-start.1 = (bf16[128,2048]{1,0:T(8,128)(2,1)S(1)}, bf16[128,2048]{1,0:T(8,128)(2,1)}, u32[]{:S(2)}) copy-start(bf16[128,2048]{1,0:T(8,128)(2,1)} %acts.1) | copy-start | bytes 1572868
  75.7 1.2 %copy-start.2 = (bf16[3,2,4,4,16,512]{5,4,3,2,1,0:T(8,128)(2,1)}, bf16[3,2,4,4,16,512]{5,4,3,2,1,0:T(8,128)(2,1)S(1)}, u32[]{:S(2)}) copy-start(bf16[3,2,4,4,16,512]{5,4,3,2,1,0:T(8,128)(2,1)S(1)} %get-tuple-element.9) | copy-start | bytes 4718596
  75.7 1.3 %copy-start.7 = (bf16[8,128,256]{2,1,0:T(8,128)(2,1)}, bf16[8,128,256]{2,1,0:T(8,128)(2,1)S(1)}, u32[]{:S(2)}) copy-start(bf16[8,128,256]{2,1,0:T(8,128)(2,1)S(1)} %get-tuple-element.10) | copy-start | bytes 1572868
  77.0 1.7 %copy-start.8 = (bf16[8,128,256]{2,1,0:T(8,128)(2,1)S(1)}, bf16[8,128,256]{2,1,0:T(8,128)(2,1)}, u32[]{:S(2)}) copy-start(bf16[8,128,256]{2,1,0:T(8,128)(2,1)} %copy-done.7) | copy-start | bytes 1572868
  78.6 1.2 %copy-start.4 = (f32[64,3584]{1,0:T(8,128)S(1)}, f32[64,3584]{1,0:T(8,128)}, u32[]{:S(2)}) copy-start(f32[64,3584]{1,0:T(8,128)} %first_moment.1) | copy-start | bytes 2752516
  79.9 1.2 %copy-start.5 = (f32[64,3584]{1,0:T(8,128)S(1)}, f32[64,3584]{1,0:T(8,128)}, u32[]{:S(2)}) copy-start(f32[64,3584]{1,0:T(8,128)} %second_moment.1) | copy-start | bytes 2752516
  81.0 0.9 %copy-start.6 = (bf16[512,256]{1,0:T(8,128)(2,1)S(1)}, bf16[512,256]{1,0:T(8,128)(2,1)}, u32[]{:S(2)}) copy-start(bf16[512,256]{1,0:T(8,128)(2,1)} %fusion.3) | copy-start | bytes 786436
